TPU v7x, 32 devices: a whole 2x2x4 slice. The times are simulated.
32 devices in a mesh: row: 8 (over z, y), col: 4 (over x, core).
Axes of the slice: x: 2, y: 2, z: 4, core: 2. Of those that a mesh axis runs over, the one named last changes fastest.
Arguments:
- leaf_grad: bfloat16 [32, 32, 1024], P('row', None, 'col'), may hold values from -6 to 6
- leaf_inv: bfloat16 [32, 1024, 1024], P('row', 'col'), as said below
- leaf_cpl: bfloat16 [32, 1024, 512], P('row', 'col'), may hold values from -0.125 to 0.125
- leaf_size: int32 [32], P('row'), may hold values from 256 to 1024, as said below
- leaf_parent: int32 [32], P('row'), may hold values from 0 to 3
- leaf_map: int32 [32, 512], P('row'), may hold values from 0 to 2047
- mid_grad: bfloat16 [32, 4, 2048], P(None, 'col', 'row'), may hold values from -6 to 6
- mid_inv: bfloat16 [4, 2048, 2048], P('col', 'row'), as said below
- mid_cpl: bfloat16 [4, 2048, 512], P('col', 'row'), may hold values from -0.125 to 0.125
- mid_map: int32 [4, 512], replicated, may hold values from 0 to 2047
- root_grad: bfloat16 [32, 2048], P(None, 'row'), may hold values from -6 to 6
- root_inv: bfloat16 [2048, 2048], P('row'), as said below
Outputs:
- leaf_x: float32 [32, 32, 1024], P('row', None, 'col')
- mid_x: float32 [32, 4, 2048], P(None, 'col', 'row')
- root_x: float32 [32, 2048], P(None, 'row')
Inputs may be any that keep to these rules, and one draw needn't show every extreme that they name: `leaf_size`: some leaf in every draw has 1024 live pivot columns. `leaf_map`: columns may repeat. `mid_map`: columns may repeat. `leaf_inv`: upper triangular; diagonal entries between 1 and 1.25, entries above the diagonal of scale 1024 ** -0.5. `mid_inv`: each front's block is upper triangular; diagonal entries between 1 and 1.25, entries above the diagonal of scale 2048 ** -0.5. `root_inv`: upper triangular; diagonal entries between 1 and 1.25, entries above the diagonal of scale 2048 ** -0.5.
All inputs are finite; a program needn't handle non-finite values.
Results may differ from a plain program's by a relative error of at most 0.012.
Values may be sent and summed in bfloat16 or wider, within the bound.
A program may use at most 64 MiB of HBM per device.

v0:
```python
import jax
import jax.numpy as jnp
from jax import lax
from jax.sharding import PartitionSpec as P


def body(
    leaf_grad,
    leaf_inv,
    leaf_cpl,
    leaf_size,
    leaf_parent,
    leaf_map,
    mid_grad,
    mid_inv,
    mid_cpl,
    mid_map,
    root_grad,
    root_inv,
):
    ncolumns = lax.axis_size("col")
    row_id = lax.axis_index("row")
    col_id = lax.axis_index("col")
    nleaves = leaf_inv.shape[0]
    share_rows = leaf_inv.shape[1]
    nrhs = leaf_grad.shape[1]
    front = mid_inv.shape[2]
    mid_rows = mid_inv.shape[1]
    nmiddle = mid_map.shape[0]
    root_order = root_inv.shape[1]
    root_rows = root_inv.shape[0]
    inv_block = mid_inv[0]
    cpl_block = mid_cpl[0]
    first_cols = col_id * share_rows + lax.iota(jnp.int32, share_rows)
    live = (first_cols[None, :] < leaf_size[:, None])[:, None, :]
    partial_value = jnp.einsum(
        "lkp,lpq->lkq", leaf_grad, leaf_inv, preferred_element_type=jnp.float32
    )
    leaf_y = jnp.where(
        live, lax.psum_scatter(partial_value, "col", scatter_dimension=2, tiled=True), 0.0
    )
    leaf_yb = leaf_y.astype(jnp.bfloat16)
    shares = jnp.einsum("lkp,lpc->klc", leaf_yb, leaf_cpl, preferred_element_type=jnp.float32)
    placed_cols = (
        leaf_map // mid_rows * ncolumns + leaf_parent[:, None]
    ) * mid_rows + leaf_map % mid_rows
    targets = placed_cols.reshape(-1)
    spread = (
        jnp.zeros((nrhs, nmiddle * front), jnp.float32).at[:, targets].add(shares.reshape(nrhs, -1))
    )
    arrived = lax.psum_scatter(spread, ("row", "col"), scatter_dimension=1, tiled=True)
    mid_hb = (mid_grad[:, 0, :].astype(jnp.float32) - arrived).astype(jnp.bfloat16)
    mid_part = jnp.dot(mid_hb, inv_block, preferred_element_type=jnp.float32)
    mid_y = lax.psum_scatter(mid_part, "row", scatter_dimension=1, tiled=True)
    mid_yb = mid_y.astype(jnp.bfloat16)
    mid_share = jnp.dot(mid_yb, cpl_block, preferred_element_type=jnp.float32)
    root_cols = lax.dynamic_index_in_dim(mid_map, col_id, 0, keepdims=False)
    root_term = jnp.zeros((nrhs, root_order), jnp.float32).at[:, root_cols].add(mid_share)
    root_total = lax.psum(root_term, ("row", "col"))
    root_slice = lax.dynamic_slice_in_dim(root_total, row_id * root_rows, root_rows, 1)
    root_hb = (root_grad.astype(jnp.float32) - root_slice).astype(jnp.bfloat16)
    root_y = lax.psum(jnp.dot(root_hb, root_inv, preferred_element_type=jnp.float32), "row")
    root_yb = root_y.astype(jnp.bfloat16)
    root_x = jnp.einsum("kq,pq->kp", root_yb, root_inv, preferred_element_type=jnp.float32)
    root_all = lax.all_gather(root_x.astype(jnp.bfloat16), "row", axis=1, tiled=True)
    coupled = root_all[:, root_cols]
    mid_wb = (
        mid_y - jnp.einsum("kc,bc->kb", coupled, cpl_block, preferred_element_type=jnp.float32)
    ).astype(jnp.bfloat16)
    full_w = lax.all_gather(mid_wb, "row", axis=1, tiled=True)
    mid_x = jnp.einsum("kq,bq->kb", full_w, inv_block, preferred_element_type=jnp.float32)
    all_mid = lax.all_gather(mid_x.astype(jnp.bfloat16), ("row", "col"), axis=1, tiled=True)
    picked = all_mid[:, targets].reshape(nrhs, nleaves, -1)
    leaf_w = leaf_y - jnp.einsum(
        "klc,lpc->lkp", picked, leaf_cpl, preferred_element_type=jnp.float32
    )
    leaf_wb = jnp.where(live, leaf_w, 0.0).astype(jnp.bfloat16)
    leaf_x = jnp.einsum(
        "lkq,lpq->lkp",
        lax.all_gather(leaf_wb, "col", axis=2, tiled=True),
        leaf_inv,
        preferred_element_type=jnp.float32,
    )
    return (leaf_x, mid_x[:, None, :], root_x)


def solution(mesh):
    placed = (
        P("row", None, "col"),
        P("row", "col", None),
        P("row", "col", None),
        P("row"),
        P("row"),
        P("row", None),
        P(None, "col", "row"),
        P("col", "row", None),
        P("col", "row", None),
        P(),
        P(None, "row"),
        P("row", None),
    )
    return jax.shard_map(
        body,
        mesh=mesh,
        in_specs=placed,
        out_specs=(P("row", None, "col"), P(None, "col", "row"), P(None, "row")),
        check_vma=False,
    )
```

profile of v0, /device:TPU:0, one launch (start us, length us, event | category | flops | bytes accessed | tf_op | source)
XLA Modules:
  0.0 564.7 jit_solution(4328340582519329368)
XLA Ops:
  7.2 0.0 copy-start
  7.2 0.0 copy-start.2
  7.2 0.0 reduce-scatter.4.cloned.1.call-start
  7.3 1.5 copy-done
  8.8 2.1 fusion.33
  10.9 0.0 reduce-scatter.4.cloned.1.call-update
  10.9 0.0 reduce-scatter.6.cloned.1.call-start
  10.9 0.0 copy-done.8
  11.0 0.0 copy-done.9
  11.0 0.1 fusion.26
  11.1 0.1 broadcast_compare_fusion
  11.2 24.2 %reduce-scatter.4.cloned.1.call-done = f32[4,32,256]{2,1,0:T(8,128)} async-done(((f32[4,32,1024]{2,1,0:T(8,128)}), f32[4,32,256]{2,1,0:T(8,128)}) %reduce-scatter.4.cloned.1.call-update) | async-done | bytes 131088 | tf_op jit(solution)/shard_map/reduce_scatter | solution.py:40
  35.4 1.2 convolution_bitcast_fusion
  36.6 0.3 copy.22
  36.9 13.6 %scatter_custom_fusion = f32[32,8192]{0,1:T(8,128)} fusion(s32[2048]{0:T(1024)S(1)} %bitcast.54, f32[2048,32]{1,0:T(8,128)S(1)} %copy.22, f32[]{:T(128)} %constant.45.clone.1), kind=kCustom, calls=%fused_computation.4 | custom fusion | flops 65536 | bytes 1048580 | tf_op jit(solution)/shard_map/scatter-add | solution.py:49
  50.6 0.0 reduce-scatter.6.cloned.1.call-update
  50.6 0.0 reduce-scatter.8.cloned.1.call-start
  50.6 0.6 copy-done.6
  51.3 0.1 copy.20
  51.4 0.0 copy-start.1
  51.4 140.2 %reduce-scatter.6.cloned.1.call-done = f32[32,256]{0,1:T(8,128)} async-done(((f32[32,8192]{0,1:T(8,128)}), f32[32,256]{0,1:T(8,128)}) %reduce-scatter.6.cloned.1.call-update) | async-done | bytes 32784 | tf_op jit(solution)/shard_map/reduce_scatter | solution.py:51
  191.6 2.3 fusion.7
  193.9 0.0 reduce-scatter.8.cloned.1.call-update
  194.0 0.0 all-reduce.3.cloned.1.call-start
  194.0 0.7 compare_select_fusion.1
  194.7 58.2 %reduce-scatter.8.cloned.1.call-done = f32[32,256]{1,0:T(8,128)} async-done(((f32[32,2048]{1,0:T(8,128)}), f32[32,256]{1,0:T(8,128)}) %reduce-scatter.8.cloned.1.call-update) | async-done | bytes 32784 | tf_op jit(solution)/shard_map/reduce_scatter | solution.py:54
  252.9 1.7 convolution_bitcast_fusion.1
  254.6 3.7 scatter_custom_fusion.1
  258.3 0.0 all-reduce.3.cloned.1.call-update
  258.4 0.1 copy.23
  258.5 129.1 %all-reduce.3.cloned.1.call-done = f32[32,2048]{0,1:T(8,128)} async-done(((f32[32,2048]{0,1:T(8,128)}), f32[32,2048]{0,1:T(8,128)}) %all-reduce.3.cloned.1.call-update) | async-done | bytes 262160 | tf_op jit(solution)/shard_map/psum | solution.py:59
  387.6 1.9 fusion.16
  389.5 39.5 %all-reduce.4 = bf16[32,2048]{1,0:T(8,128)(2,1)S(1)} all-reduce(f32[32,2048]{1,0:T(8,128)} %fusion.16), channel_id=1, replica_groups=mesh['row'=8,'col'=4] {'row'}, use_global_device_ids=true, to_apply=%region_6.7 | all-reduce | flops 65536 | bytes 393216 | tf_op jit(solution)/shard_map/psum | solution.py:62
  429.0 1.0 fusion.31
  430.0 30.5 %all_gather.12 = bf16[32,2048]{1,0:T(8,128)(2,1)S(1)} all-gather(bf16[32,256]{1,0:T(8,128)(2,1)S(1)} %get-tuple-element.9), channel_id=1, replica_groups=mesh['row'=8,'col'=4] {'row'}, dimensions={1}, use_global_device_ids=true | all-gather | bytes 147456 | tf_op jit(solution)/shard_map/all_gather | solution.py:65
  460.5 0.3 copy.24
  460.8 1.3 gather_fusion
  462.2 0.9 fusion.4
  463.1 30.5 %all_gather.13 = bf16[32,2048]{1,0:T(8,128)(2,1)S(1)} all-gather(bf16[32,256]{1,0:T(8,128)(2,1)S(1)} %fusion.4), channel_id=1, replica_groups=mesh['row'=8,'col'=4] {'row'}, dimensions={1}, use_global_device_ids=true | all-gather | bytes 147456 | tf_op jit(solution)/shard_map/all_gather | solution.py:70
  493.6 1.6 fusion.32
  495.3 0.0 copy-start.3
  495.3 41.3 %all_gather.14 = bf16[32,8192]{1,0:T(8,128)(2,1)} all-gather(bf16[32,256]{1,0:T(8,128)(2,1)S(1)} %get-tuple-element.11), channel_id=1, replica_groups=mesh['row'=8,'col'=4] {'row','col'}, dimensions={1}, use_global_device_ids=true | all-gather | bytes 540672 | tf_op jit(solution)/shard_map/all_gather | solution.py:72
  536.6 2.7 copy.25
  539.3 9.5 %gather_fusion.1 = bf16[2048,32]{1,0:T(8,128)(2,1)} fusion(bf16[32,8192]{0,1:T(8,128)(2,1)} %copy.25, s32[2048]{0:T(1024)S(1)} %broadcast_clamp_fusion), kind=kCustom, calls=%fused_computation.1 | custom fusion | bytes 270336 | tf_op jit(solution)/shard_map/gather | solution.py:73
  548.8 1.5 fusion.3
  550.3 5.9 %all_gather.15 = bf16[4,32,1024]{2,1,0:T(8,128)(2,1)S(1)} all-gather(bf16[4,32,256]{2,1,0:T(8,128)(2,1)S(1)} %fusion.3), channel_id=1, replica_groups=mesh['row'=8,'col'=4] {'col'}, dimensions={2}, use_global_device_ids=true | all-gather | bytes 327680 | tf_op jit(solution)/shard_map/all_gather | solution.py:80
  556.2 1.4 fusion.34
  557.6 0.6 copy.26
  (20 shorter events, 0.1 us)
Async XLA Ops:
  7.2 1.6 copy-start
  7.2 3.8 copy-start.8
  7.2 3.8 copy-start.9
  7.2 3.9 copy-start.10
  7.2 28.2 %copy-start.2 = (bf16[4,256,512]{2,1,0:T(8,128)(2,1)S(1)}, bf16[4,256,512]{2,1,0:T(8,128)(2,1)}, u32[]{:S(2)}) copy-start(bf16[4,256,512]{2,1,0:T(8,128)(2,1)} %param.14) | copy-start | bytes 3145732
  7.2 28.2 %reduce-scatter.4.cloned.1.call-start = ((), (), s32[]{:S(2)}) async-start(), calls=%async_computation.3 | async-start | bytes 655360 | tf_op jit(solution)/shard_map/reduce_scatter | solution.py:40
  10.9 180.7 %reduce-scatter.6.cloned.1.call-start = ((), (), s32[]{:S(2)}) async-start(), calls=%async_computation.4 | async-start | bytes 4325376 | tf_op jit(solution)/shard_map/reduce_scatter | solution.py:51
  50.6 0.7 copy-start.6
  50.6 202.4 %copy-start.4 = (bf16[1,256,512]{2,1,0:T(8,128)(2,1)S(1)}, bf16[1,256,512]{2,1,0:T(8,128)(2,1)}, u32[]{:S(2)}) copy-start(bf16[1,256,512]{2,1,0:T(8,128)(2,1)} %param.20) | copy-start | bytes 786436
  50.6 202.3 %reduce-scatter.8.cloned.1.call-start = ((), (), s32[]{:S(2)}) async-start(), calls=%async_computation.5 | async-start | bytes 294912 | tf_op jit(solution)/shard_map/reduce_scatter | solution.py:54
  51.4 207.0 %copy-start.7 = (bf16[32,256]{1,0:T(8,128)(2,1)S(1)}, bf16[32,256]{1,0:T(8,128)(2,1)}, u32[]{:S(2)}) copy-start(bf16[32,256]{1,0:T(8,128)(2,1)} %param.22) | copy-start | bytes 49156
  51.4 336.2 %copy-start.1 = (bf16[256,2048]{1,0:T(8,128)(2,1)S(1)}, bf16[256,2048]{1,0:T(8,128)(2,1)}, u32[]{:S(2)}) copy-start(bf16[256,2048]{1,0:T(8,128)(2,1)} %param.23) | copy-start | bytes 3145732
  194.0 193.7 %all-reduce.3.cloned.1.call-start = ((), (), s32[]{:S(2)}) async-start(), calls=%async_computation.6 | async-start | bytes 2097152 | tf_op jit(solution)/shard_map/psum | solution.py:59
  495.3 53.5 %copy-start.3 = (bf16[4,256,512]{2,1,0:T(8,128)(2,1)S(1)}, bf16[4,256,512]{2,1,0:T(8,128)(2,1)}, u32[]{:S(2)}) copy-start(bf16[4,256,512]{2,1,0:T(8,128)(2,1)} %param.14) | copy-start | bytes 3145732
  495.3 53.5 %copy-start.5 = (f32[4,32,256]{2,1,0:T(8,128)S(1)}, f32[4,32,256]{2,1,0:T(8,128)}, u32[]{:S(2)}) copy-start(f32[4,32,256]{2,1,0:T(8,128)} %reduce-scatter.4.cloned.1.call-done) | copy-start | bytes 393220
Sparse Core Ops, SparseCore 0:
  11.0 24.3 reduce-scatter.3
  50.7 140.8 reduce-scatter.5
  195.3 57.5 reduce-scatter.7
  258.8 128.7 all-reduce.2
where the time goes:
time: 565 us
  waiting for transfers between devices  352 us (62%)
  blocking collectives  148 us (26%)
  other arithmetic  18.2 us (3%)
  local copies, waits for them, and re-layouts  17.3 us (3%)
  matrix products  15.7 us (3%)
  between operations  14 us (2%)
    reduce_scatter x1, waiting for transfers between devices, body(): lax.psum_scatter(spread, ('row', 'col'), scatter_dimension=1, tiled=True)  140 us
    psum x1, waiting for transfers between devices, body(): root_total = lax.psum(root_term, ('row', 'col'))  129 us
    reduce_scatter x1, waiting for transfers between devices, body(): mid_y = lax.psum_scatter(mid_part, 'row', scatter_dimension=1, tiled=True)  58.2 us
    all_gather x1, blocking collectives, body(): lax.all_gather(mid_x.astype(jnp.bfloat16), ('row', 'col'), axis=1, tiled=...  41.3 us
    psum x1, blocking collectives, body(): lax.psum(jnp.dot(root_hb, root_inv, preferred_element_type=jnp.float32),...  39.5 us
    all_gather x1, blocking collectives, body(): full_w = lax.all_gather(mid_wb, 'row', axis=1, tiled=True)  30.5 us
    all_gather x1, blocking collectives, body(): lax.all_gather(root_x.astype(jnp.bfloat16), 'row', axis=1, tiled=True)  30.5 us
    reduce_scatter x1, waiting for transfers between devices, body(): lax.psum_scatter(partial_value, 'col', scatter_dimension=2, tiled=True)  24.2 us
  transfers between devices with their start and end apart: 4, of which 4 were waited for; matrix products, arithmetic and copies ran while one was open for 0% of the time, Pallas kernels for 0%

commit v1 on v0

--- a/solution.py
+++ b/solution.py
@@ -1,7 +1,437 @@
+import functools
+
 import jax
 import jax.numpy as jnp
 from jax import lax
+from jax.experimental import pallas as pl
+from jax.experimental.pallas import tpu as pltpu
 from jax.sharding import PartitionSpec as P
+
+MESH = pl.DeviceIdType.MESH
+F32 = jnp.float32
+BF16 = jnp.bfloat16
+LANES = 128
+
+
+def dot(a, b):
+    return jnp.dot(a, b, preferred_element_type=F32)
+
+
+def dot_t(a, b):
+    return lax.dot_general(a, b, (((1,), (1,)), ((), ())), preferred_element_type=F32)
+
+
+def pack(x):
+    return jnp.concatenate(
+        [x[:, i : i + LANES] for i in range(0, x.shape[1], LANES)], axis=0
+    )
+
+
+def kernel(
+    nrow,
+    ncol,
+    grad_ref,
+    inv_hbm,
+    cpl_hbm,
+    size_ref,
+    parent_ref,
+    map_ref,
+    mgrad_ref,
+    minv_hbm,
+    mcpl_hbm,
+    mmap_ref,
+    rgrad_ref,
+    rinv_hbm,
+    leaf_out,
+    mid_out,
+    root_out,
+    inv,
+    cpl,
+    minv,
+    mcpl,
+    rinv,
+    pick,
+    mpick,
+    leaf_y,
+    rgrad,
+    s_fwd,
+    r_fwd,
+    s_cpl,
+    r_cpl,
+    s_con,
+    r_con,
+    s_mid,
+    r_mid,
+    s_root,
+    r_root,
+    s_ry,
+    r_ry,
+    s_rg,
+    r_rg,
+    s_rx,
+    r_rx,
+    s_mw,
+    r_mw,
+    s_mx,
+    r_mx,
+    s_pk,
+    r_pk,
+    s_lw,
+    r_lw,
+    load_sem,
+    send_sem,
+    recv_sem,
+):
+    ndev = nrow * ncol
+    row, col = lax.axis_index("row"), lax.axis_index("col")
+    me = row * ncol + col
+    nleaf, nrhs, share = grad_ref.shape
+    kc = nrhs // ncol
+    front = minv.shape[1]
+    width = minv.shape[0]
+    ccols = cpl.shape[2]
+    halves = width // LANES
+
+    loads = [
+        pltpu.make_async_copy(src, dst, load_sem.at[i])
+        for i, (src, dst) in enumerate(
+            [(inv_hbm, inv), (cpl_hbm, cpl), (minv_hbm, minv), (mcpl_hbm, mcpl), (rinv_hbm, rinv)]
+        )
+    ]
+    for load in loads:
+        load.start()
+
+    barrier = pltpu.get_barrier_semaphore()
+
+    def greet(t, _):
+        other = lax.rem(me + t, ndev)
+        pl.semaphore_signal(
+            barrier,
+            inc=1,
+            device_id=(lax.div(other, ncol), lax.rem(other, ncol)),
+            device_id_type=MESH,
+        )
+        return 0
+
+    lax.fori_loop(1, ndev, greet, 0)
+
+    def to_all(phase, src_of, dst):
+        def step(t, _):
+            other = lax.rem(me + t, ndev)
+            orow, ocol = lax.div(other, ncol), lax.rem(other, ncol)
+            pltpu.make_async_remote_copy(
+                src_ref=src_of(other, ocol),
+                dst_ref=dst.at[me],
+                send_sem=send_sem.at[phase],
+                recv_sem=recv_sem.at[phase],
+                device_id=(orow, ocol),
+                device_id_type=MESH,
+            ).start()
+            return 0
+
+        lax.fori_loop(1, ndev, step, 0)
+
+    def to_rows(phase, src_of, dst):
+        def step(t, _):
+            orow = lax.rem(row + t, nrow)
+            pltpu.make_async_remote_copy(
+                src_ref=src_of(orow),
+                dst_ref=dst.at[row],
+                send_sem=send_sem.at[phase],
+                recv_sem=recv_sem.at[phase],
+                device_id=(orow, col),
+                device_id_type=MESH,
+            ).start()
+            return 0
+
+        lax.fori_loop(1, nrow, step, 0)
+
+    def to_cols(phase, src_of, dst):
+        def step(t, _):
+            ocol = lax.rem(col + t, ncol)
+            pltpu.make_async_remote_copy(
+                src_ref=src_of(ocol),
+                dst_ref=dst.at[col],
+                send_sem=send_sem.at[phase],
+                recv_sem=recv_sem.at[phase],
+                device_id=(row, ocol),
+                device_id_type=MESH,
+            ).start()
+            return 0
+
+        lax.fori_loop(1, ncol, step, 0)
+
+    def arrive(phase, dst):
+        part = dst.at[pl.ds(0, dst.shape[0] - 1)]
+        pltpu.make_async_copy(part, part, recv_sem.at[phase]).wait()
+
+    def sent(phase, dst):
+        part = dst.at[pl.ds(0, dst.shape[0] - 1)]
+        pltpu.make_async_copy(part, part, send_sem.at[phase]).wait()
+
+    def stage_blocks(buf, t):
+        for r in range(nrow):
+            for c in range(ncol):
+                buf[r * ncol + c] = pack(
+                    t[c * kc : (c + 1) * kc, r * width : (r + 1) * width]
+                ).astype(BF16)
+
+    def unpack_all(buf):
+        x = buf[...].astype(F32)
+        x = x.reshape(nrow, ncol, halves, kc, LANES)
+        return jnp.concatenate(
+            [
+                x[r, :, h].reshape(ncol * kc, LANES)
+                for r in range(nrow)
+                for h in range(halves)
+            ],
+            axis=1,
+        ).astype(BF16)
+
+    loads[0].wait()
+    for f in range(nleaf):
+        part = dot(grad_ref[f], inv[f])
+        for c in range(ncol):
+            s_fwd[c, f] = part[:, c * share : (c + 1) * share].astype(BF16)
+    pl.semaphore_wait(barrier, ndev - 1)
+    to_cols(0, lambda c: s_fwd.at[c], r_fwd)
+    r_fwd[col] = s_fwd[col]
+
+    step_rows = 256
+
+    def fill(i, _):
+        rows = pl.ds(pl.multiple_of(i * step_rows, step_rows), step_rows)
+        ids = lax.broadcasted_iota(jnp.int32, (step_rows, ccols), 0) + i * step_rows
+        for f in range(nleaf):
+            pick[rows, f * ccols : (f + 1) * ccols] = jnp.where(
+                ids == map_ref[f : f + 1, :], 1.0, 0.0
+            ).astype(BF16)
+        return 0
+
+    lax.fori_loop(0, front // step_rows, fill, 0)
+    rgrad[...] = rgrad_ref[...].astype(F32)
+    loads[1].wait()
+
+    arrive(0, r_fwd)
+    firsts = col * share + lax.broadcasted_iota(jnp.int32, (nrhs, share), 1)
+    shares = []
+    for f in range(nleaf):
+        y = r_fwd[0, f].astype(F32)
+        for c in range(1, ncol):
+            y = y + r_fwd[c, f].astype(F32)
+        y = jnp.where(firsts < size_ref[f], y, 0.0)
+        leaf_y[f] = y
+        shares.append(dot(y.astype(BF16), cpl[f]))
+    for c in range(ncol):
+        s_cpl[c] = jnp.concatenate(
+            [u[c * kc : (c + 1) * kc] for u in shares], axis=0
+        ).astype(BF16)
+    to_cols(1, lambda c: s_cpl.at[c], r_cpl)
+    r_cpl[col] = s_cpl[col]
+
+    def fill_mid(i, _):
+        rows = pl.ds(pl.multiple_of(i * step_rows, step_rows), step_rows)
+        ids = lax.broadcasted_iota(jnp.int32, (step_rows, ccols), 0) + i * step_rows
+        mpick[rows, :] = jnp.where(ids == mmap_ref[pl.ds(col, 1), :], 1.0, 0.0).astype(BF16)
+        return 0
+
+    lax.fori_loop(0, front // step_rows, fill_mid, 0)
+    loads[2].wait()
+    loads[3].wait()
+    loads[4].wait()
+
+    arrive(1, r_cpl)
+    u = r_cpl[0].astype(F32)
+    for c in range(1, ncol):
+        u = u + r_cpl[c].astype(F32)
+    spread = jnp.concatenate(
+        [
+            jnp.concatenate(
+                [
+                    jnp.where(parent_ref[f] == p, u[f * kc : (f + 1) * kc], 0.0)
+                    for p in range(ncol)
+                ],
+                axis=0,
+            )
+            for f in range(nleaf)
+        ],
+        axis=1,
+    ).astype(BF16)
+    stage_blocks(s_con, dot_t(spread, pick[...]))
+    to_all(2, lambda d, c: s_con.at[d], r_con)
+    r_con[me] = s_con[me]
+
+    arrive(2, r_con)
+    got = r_con[...].astype(F32).reshape(nrow, ncol, halves, kc, LANES)
+    total = got[0]
+    for r in range(1, nrow):
+        total = total + got[r]
+    contrib = jnp.concatenate(
+        [total[:, h].reshape(nrhs, LANES) for h in range(halves)], axis=1
+    )
+    mid_hb = (mgrad_ref[...].astype(F32) - contrib).astype(BF16)
+    part = dot(mid_hb, minv[...])
+    for r in range(nrow):
+        s_mid[r] = part[:, r * width : (r + 1) * width].astype(BF16)
+    to_rows(3, lambda r: s_mid.at[r], r_mid)
+    r_mid[row] = s_mid[row]
+    arrive(3, r_mid)
+    mid_y = r_mid[0].astype(F32)
+    for r in range(1, nrow):
+        mid_y = mid_y + r_mid[r].astype(F32)
+
+    mid_u = dot(mid_y.astype(BF16), mcpl[...])
+    stage_blocks(s_root, dot_t(mid_u.astype(BF16), mpick[...]))
+    to_all(4, lambda d, c: s_root.at[d], r_root)
+    r_root[me] = s_root[me]
+    arrive(4, r_root)
+    total = jnp.sum(r_root[...].astype(F32), axis=0)
+    root_total = jnp.concatenate(
+        [total[h * kc : (h + 1) * kc] for h in range(halves)], axis=1
+    )
+    mine = rgrad[pl.ds(pl.multiple_of(col * kc, kc), kc), :]
+    root_hb = (mine - root_total).astype(BF16)
+    part = dot(root_hb, rinv[...])
+    for r in range(nrow):
+        s_ry[r] = pack(part[:, r * width : (r + 1) * width]).astype(BF16)
+    to_rows(5, lambda r: s_ry.at[r], r_ry)
+    r_ry[row] = s_ry[row]
+    arrive(5, r_ry)
+    s_rg[...] = jnp.sum(r_ry[...].astype(F32), axis=0).astype(BF16)
+    to_rows(6, lambda r: s_rg, r_rg)
+    r_rg[row] = s_rg[...]
+    arrive(6, r_rg)
+    ry = r_rg[...].astype(F32)
+    root_yb = jnp.concatenate(
+        [ry[r, h * kc : (h + 1) * kc] for r in range(nrow) for h in range(halves)], axis=1
+    ).astype(BF16)
+    s_rx[...] = pack(dot_t(root_yb, rinv[...])).astype(BF16)
+    to_all(7, lambda d, c: s_rx, r_rx)
+    r_rx[me] = s_rx[...]
+    arrive(7, r_rx)
+    root_xb = unpack_all(r_rx)
+    own = r_rx[pl.ds(row * ncol, ncol)].astype(F32).reshape(ncol, halves, kc, LANES)
+    for h in range(halves):
+        root_out[:, h * LANES : (h + 1) * LANES] = own[:, h].reshape(nrhs, LANES)
+
+    coupled = dot(root_xb, mpick[...]).astype(BF16)
+    s_mw[...] = (mid_y - dot_t(coupled, mcpl[...])).astype(BF16)
+    to_rows(8, lambda r: s_mw, r_mw)
+    r_mw[row] = s_mw[...]
+    arrive(8, r_mw)
+    full_w = jnp.concatenate([r_mw[r] for r in range(nrow)], axis=1)
+    mid_x = dot_t(full_w, minv[...])
+    mid_out[...] = mid_x
+    for c in range(ncol):
+        s_mx[c] = pack(mid_x[c * kc : (c + 1) * kc]).astype(BF16)
+    to_all(9, lambda d, c: s_mx.at[c], r_mx)
+    r_mx[me] = s_mx[col]
+    arrive(9, r_mx)
+
+    every = dot(unpack_all(r_mx), pick[...])
+    picked = []
+    for f in range(nleaf):
+        cols = slice(f * ccols, (f + 1) * ccols)
+        x = jnp.where(parent_ref[f] == 0, every[0:kc, cols], 0.0)
+        for p in range(1, ncol):
+            x = jnp.where(parent_ref[f] == p, every[p * kc : (p + 1) * kc, cols], x)
+        picked.append(x)
+    s_pk[...] = jnp.concatenate(picked, axis=0).astype(BF16)
+    to_cols(10, lambda c: s_pk, r_pk)
+    r_pk[col] = s_pk[...]
+    arrive(10, r_pk)
+
+    got = r_pk[...].astype(F32)
+    for f in range(nleaf):
+        xb = jnp.concatenate(
+            [got[c, f * kc : (f + 1) * kc] for c in range(ncol)], axis=0
+        ).astype(BF16)
+        w = leaf_y[f] - dot_t(xb, cpl[f])
+        s_lw[f] = jnp.where(firsts < size_ref[f], w, 0.0).astype(BF16)
+    to_cols(11, lambda c: s_lw, r_lw)
+    r_lw[col] = s_lw[...]
+    arrive(11, r_lw)
+    for f in range(nleaf):
+        w = jnp.concatenate([r_lw[c, f] for c in range(ncol)], axis=1)
+        leaf_out[f] = dot_t(w, inv[f])
+
+    for phase, buf in enumerate(
+        [r_fwd, r_cpl, r_con, r_mid, r_root, r_ry, r_rg, r_rx, r_mw, r_mx, r_pk, r_lw]
+    ):
+        sent(phase, buf)
+
+
+def fused(nrow, ncol, *args):
+    (leaf_grad, leaf_inv, leaf_cpl, leaf_size, leaf_parent, leaf_map, mid_grad, mid_inv,
+     mid_cpl, mid_map, root_grad, root_inv) = args
+    nleaf, nrhs, share = leaf_grad.shape
+    order = leaf_inv.shape[2]
+    ccols = leaf_cpl.shape[2]
+    width, front = mid_inv.shape[1:]
+    ndev, kc, halves = nrow * ncol, nrhs // ncol, width // LANES
+    vmem = pl.BlockSpec(memory_space=pltpu.VMEM)
+    smem = pl.BlockSpec(memory_space=pltpu.SMEM)
+    anyw = pl.BlockSpec(memory_space=pl.ANY)
+    block = (halves * kc, LANES)
+    scratch = [
+        ((nleaf, share, order), BF16),
+        ((nleaf, share, ccols), BF16),
+        ((width, front), BF16),
+        ((width, mid_cpl.shape[2]), BF16),
+        (root_inv.shape, BF16),
+        ((front, nleaf * ccols), BF16),
+        ((root_inv.shape[1], mid_cpl.shape[2]), BF16),
+        ((nleaf, nrhs, share), F32),
+        (root_grad.shape, F32),
+        ((ncol, nleaf, nrhs, share), BF16),
+        ((ncol, nleaf, nrhs, share), BF16),
+        ((ncol, nleaf * kc, ccols), BF16),
+        ((ncol, nleaf * kc, ccols), BF16),
+        ((ndev, *block), BF16),
+        ((ndev, *block), BF16),
+        ((nrow, nrhs, width), BF16),
+        ((nrow, nrhs, width), BF16),
+        ((ndev, *block), BF16),
+        ((ndev, *block), BF16),
+        ((nrow, *block), BF16),
+        ((nrow, *block), BF16),
+        (block, BF16),
+        ((nrow, *block), BF16),
+        (block, BF16),
+        ((ndev, *block), BF16),
+        ((nrhs, width), BF16),
+        ((nrow, nrhs, width), BF16),
+        ((ncol, *block), BF16),
+        ((ndev, *block), BF16),
+        ((nleaf * kc, ccols), BF16),
+        ((ncol, nleaf * kc, ccols), BF16),
+        ((nleaf, nrhs, share), BF16),
+        ((ncol, nleaf, nrhs, share), BF16),
+    ]
+    phases = 12
+    leaf_x, mid_x, root_x = pl.pallas_call(
+        functools.partial(kernel, nrow, ncol),
+        out_shape=(
+            jax.ShapeDtypeStruct((nleaf, nrhs, share), F32),
+            jax.ShapeDtypeStruct((nrhs, width), F32),
+            jax.ShapeDtypeStruct((nrhs, width), F32),
+        ),
+        in_specs=[vmem, anyw, anyw, smem, smem, vmem, vmem, anyw, anyw, vmem, vmem, anyw],
+        out_specs=(vmem, vmem, vmem),
+        scratch_shapes=[pltpu.VMEM(shape, dtype) for shape, dtype in scratch]
+        + [
+            pltpu.SemaphoreType.DMA((5,)),
+            pltpu.SemaphoreType.DMA((phases,)),
+            pltpu.SemaphoreType.DMA((phases,)),
+        ],
+        compiler_params=pltpu.CompilerParams(
+            collective_id=0, has_side_effects=True, vmem_limit_bytes=48 * 2**20
+        ),
+    )(
+        leaf_grad, leaf_inv, leaf_cpl, leaf_size, leaf_parent, leaf_map, mid_grad[:, 0, :],
+        mid_inv[0], mid_cpl[0], mid_map, root_grad, root_inv,
+    )
+    return leaf_x, mid_x[:, None, :], root_x
 
 
 def body(
@@ -99,8 +529,18 @@
         P(None, "row"),
         P("row", None),
     )
+    nrow, ncol = mesh.shape["row"], mesh.shape["col"]
+
+    def run(*args):
+        width = args[7].shape[1]
+        whole_tiles = width % LANES == 0 and args[0].shape[1] // ncol % 8 == 0
+        one_front = args[9].shape[0] == ncol and args[11].shape[0] == width
+        if whole_tiles and one_front:
+            return fused(nrow, ncol, *args)
+        return body(*args)
+
     return jax.shard_map(
-        body,
+        run,
         mesh=mesh,
         in_specs=placed,
         out_specs=(P("row", None, "col"), P(None, "col", "row"), P(None, "row")),

time: 565 us -> 84.3 us (0.15)
  waiting for transfers between devices: 352 us -> 0 us
  blocking collectives: 148 us -> 0 us
  Pallas kernels: 0 us -> 69.7 us
  other arithmetic: 18.2 us -> 0 us
  matrix products: 15.7 us -> 0 us
  between operations: 14 us -> 0.66 us
    reduce_scatter x3 -> x0, waiting for transfers between devices: 223 us -> none  [the longest x1 140 us: body(): lax.psum_scatter(spread, ('row', 'col'), scatter_dimension=1, tiled=True)]
    psum x1 -> x0, waiting for transfers between devices: 129 us -> none  [body(): root_total = lax.psum(root_term, ('row', 'col'))]
    all_gather x4 -> x0, blocking collectives: 108 us -> none  [the longest x1 41.3 us: body(): lax.all_gather(mid_x.astype(jnp.bfloat16), ('row', 'col'), axis=1, tiled=...]
    pallas_call x0 -> x1, Pallas kernels: none -> 69.7 us  [fused(): pl.pallas_call(functools.partial(kernel, nrow, ncol), out_shape=(jax.Shap...]
    psum x1 -> x0, blocking collectives: 39.5 us -> none  [body(): lax.psum(jnp.dot(root_hb, root_inv, preferred_element_type=jnp.float32),...]
    scatter-add x2 -> x0, other arithmetic: 17.3 us -> none  [the longest x1 13.6 us: body(): jnp.zeros((nrhs, nmiddle * front), jnp.float32).at[:, targets]]
    dot_general x10 -> x0, matrix products: 15.7 us -> none  [the longest x1 2.31 us: body(): mid_part = jnp.dot(mid_hb, inv_block, preferred_element_type=jnp.float32)]
    gather x2 -> x0, local copies, waits for them, and re-layouts: 10.9 us -> none  [the longest x1 9.54 us: body(): picked = all_mid[:, targets].reshape(nrhs, nleaves, -1)]
  transfers between devices with their start and end apart: 4 -> 0, of which waited for: 4 -> 0; matrix products, arithmetic and copies ran while one was open for 0% -> 0% of each run, Pallas kernels for 0% -> 0%
where the time goes in v1:
time: 84.3 us; the launch traced here: 83.4 us
  Pallas kernels  69.7 us (83%)
  local copies, waits for them, and re-layouts  13.1 us (16%)
    pallas_call x1, Pallas kernels, fused(): pl.pallas_call(functools.partial(kernel, nrow, ncol), out_shape=(jax.Shap...  69.7 us
    unnamed x27, local copies, waits for them, and re-layouts  13.1 us

profile of v1, /device:TPU:0, one launch (start us, length us, event | category | flops | bytes accessed | tf_op | source)
XLA Modules:
  0.0 83.4 jit_solution(12833347123325955999)
XLA Ops:
  0.6 0.0 copy-start
  0.6 1.6 %copy-done = bf16[4,256,1024]{2,1,0:T(8,128)(2,1)S(1)} copy-done((bf16[4,256,1024]{2,1,0:T(8,128)(2,1)S(1)}, bf16[4,256,1024]{2,1,0:T(8,128)(2,1)}, u32[]{:S(2)}) %copy-start) | copy-done | bytes 2097176
  2.2 0.0 copy-start.1
  2.2 1.2 %copy-done.1 = bf16[4,256,512]{2,1,0:T(8,128)(2,1)S(1)} copy-done((bf16[4,256,512]{2,1,0:T(8,128)(2,1)S(1)}, bf16[4,256,512]{2,1,0:T(8,128)(2,1)}, u32[]{:S(2)}) %copy-start.1) | copy-done | bytes 1048600
  3.5 0.0 copy-start.2
  3.5 1.2 %copy-done.2 = bf16[1,256,2048]{2,1,0:T(8,128)(2,1)S(1)} copy-done((bf16[1,256,2048]{2,1,0:T(8,128)(2,1)S(1)}, bf16[1,256,2048]{2,1,0:T(8,128)(2,1)}, u32[]{:S(2)}) %copy-start.2) | copy-done | bytes 1048600
  4.7 0.0 copy-start.3
  4.7 1.2 %copy-done.3 = bf16[256,2048]{1,0:T(8,128)(2,1)S(1)} copy-done((bf16[256,2048]{1,0:T(8,128)(2,1)S(1)}, bf16[256,2048]{1,0:T(8,128)(2,1)}, u32[]{:S(2)}) %copy-start.3) | copy-done | bytes 1048600
  5.9 0.0 copy-start.4
  5.9 0.9 %copy-done.4 = bf16[1,256,512]{2,1,0:T(8,128)(2,1)S(1)} copy-done((bf16[1,256,512]{2,1,0:T(8,128)(2,1)S(1)}, bf16[1,256,512]{2,1,0:T(8,128)(2,1)}, u32[]{:S(2)}) %copy-start.4) | copy-done | bytes 262168
  6.9 0.0 copy-start.5
  6.9 0.8 %copy-done.5 = bf16[4,32,256]{2,1,0:T(8,128)(2,1)S(1)} copy-done((bf16[4,32,256]{2,1,0:T(8,128)(2,1)S(1)}, bf16[4,32,256]{2,1,0:T(8,128)(2,1)}, u32[]{:S(2)}) %copy-start.5) | copy-done | bytes 65560
  7.7 0.0 copy-start.6
  7.7 0.7 copy-done.6
  8.4 0.0 copy-start.7
  8.4 0.7 copy-done.7
  9.1 0.0 copy-start.8
  9.1 0.7 copy-done.8
  9.8 0.0 copy-start.9
  9.8 0.7 copy-done.9
  10.5 0.0 copy-start.10
  10.5 0.7 copy-done.10
  11.2 0.0 copy-start.11
  11.2 0.7 copy-done.11
  11.8 69.7 %shard_map.139 = (f32[4,32,256]{2,1,0:T(8,128)S(1)}, f32[32,256]{1,0:T(8,128)S(1)}, f32[32,256]{1,0:T(8,128)S(1)}) custom-call(bf16[4,32,256]{2,1,0:T(8,128)(2,1)S(1)} %copy-done.5, bf16[4,256,1024]{2,1,0:T(8,128)(2,1)S(1)} %copy-done, bf16[4,256,512]{2,1,0:T(8,128)(2,1)S(1)} %copy-done.1, s32[4]{0:T(128)S(1)} %copy-done.10, s32[4]{0:T(128)S(1)} %copy-done.11, ...), custom_call_target="tpu_custom_call" | custom-call | tf_op jit(solution)/shard_map/pallas_call | solution.py:412
  81.5 0.6 copy.15
  82.2 0.7 copy.18
  82.8 0.6 copy.19
Async XLA Ops:
  0.6 1.6 %copy-start = (bf16[4,256,1024]{2,1,0:T(8,128)(2,1)S(1)}, bf16[4,256,1024]{2,1,0:T(8,128)(2,1)}, u32[]{:S(2)}) copy-start(bf16[4,256,1024]{2,1,0:T(8,128)(2,1)} %inv_hbm.1) | copy-start | bytes 6291460
  2.2 1.2 %copy-start.1 = (bf16[4,256,512]{2,1,0:T(8,128)(2,1)S(1)}, bf16[4,256,512]{2,1,0:T(8,128)(2,1)}, u32[]{:S(2)}) copy-start(bf16[4,256,512]{2,1,0:T(8,128)(2,1)} %cpl_hbm.1) | copy-start | bytes 3145732
  3.5 1.2 %copy-start.2 = (bf16[1,256,2048]{2,1,0:T(8,128)(2,1)S(1)}, bf16[1,256,2048]{2,1,0:T(8,128)(2,1)}, u32[]{:S(2)}) copy-start(bf16[1,256,2048]{2,1,0:T(8,128)(2,1)} %param.19) | copy-start | bytes 3145732
  4.7 1.2 %copy-start.3 = (bf16[256,2048]{1,0:T(8,128)(2,1)S(1)}, bf16[256,2048]{1,0:T(8,128)(2,1)}, u32[]{:S(2)}) copy-start(bf16[256,2048]{1,0:T(8,128)(2,1)} %rinv_hbm.1) | copy-start | bytes 3145732
  5.9 0.9 %copy-start.4 = (bf16[1,256,512]{2,1,0:T(8,128)(2,1)S(1)}, bf16[1,256,512]{2,1,0:T(8,128)(2,1)}, u32[]{:S(2)}) copy-start(bf16[1,256,512]{2,1,0:T(8,128)(2,1)} %param.20) | copy-start | bytes 786436
  6.9 0.8 %copy-start.5 = (bf16[4,32,256]{2,1,0:T(8,128)(2,1)S(1)}, bf16[4,32,256]{2,1,0:T(8,128)(2,1)}, u32[]{:S(2)}) copy-start(bf16[4,32,256]{2,1,0:T(8,128)(2,1)} %grad_ref.1) | copy-start | bytes 196612
  7.7 0.7 copy-start.6
  8.4 0.7 copy-start.7
  9.1 0.7 copy-start.8
  9.8 0.7 copy-start.9
  10.5 0.7 copy-start.10
  11.2 0.7 copy-start.11

commit v2 on v1

--- a/solution.py
+++ b/solution.py
@@ -30,21 +30,26 @@
 def kernel(
     nrow,
     ncol,
-    grad_ref,
+    grad_hbm,
     inv_hbm,
     cpl_hbm,
-    size_ref,
-    parent_ref,
-    map_ref,
-    mgrad_ref,
+    size_hbm,
+    parent_hbm,
+    map_hbm,
+    mgrad_hbm,
     minv_hbm,
     mcpl_hbm,
-    mmap_ref,
-    rgrad_ref,
+    mmap_hbm,
+    rgrad_hbm,
     rinv_hbm,
     leaf_out,
     mid_out,
     root_out,
+    grad_ref,
+    map_ref,
+    mgrad_ref,
+    mmap_ref,
+    rgrad_ref,
     inv,
     cpl,
     minv,
@@ -78,88 +83,111 @@
     r_pk,
     s_lw,
     r_lw,
+    size_ref,
+    parent_ref,
     load_sem,
+    leaf_sem,
     send_sem,
     recv_sem,
+    send_leaf,
+    recv_leaf,
 ):
     ndev = nrow * ncol
     row, col = lax.axis_index("row"), lax.axis_index("col")
     me = row * ncol + col
     nleaf, nrhs, share = grad_ref.shape
+    loads = {
+        name: pltpu.make_async_copy(src, dst, load_sem.at[i])
+        for i, (name, src, dst) in enumerate(
+            [
+                ("grad", grad_hbm, grad_ref),
+                ("map", map_hbm, map_ref),
+                ("cpl", cpl_hbm, cpl),
+                ("size", size_hbm, size_ref),
+                ("parent", parent_hbm, parent_ref),
+                ("rgrad", rgrad_hbm, rgrad_ref),
+                ("mmap", mmap_hbm, mmap_ref),
+                ("mgrad", mgrad_hbm, mgrad_ref),
+                ("minv", minv_hbm, minv),
+                ("mcpl", mcpl_hbm, mcpl),
+                ("rinv", rinv_hbm, rinv),
+            ]
+        )
+    }
+    loads["grad"].start()
+    inv_loads = [
+        pltpu.make_async_copy(inv_hbm.at[f], inv.at[f], leaf_sem.at[f]) for f in range(nleaf)
+    ]
+    for load in inv_loads:
+        load.start()
+    for name, load in loads.items():
+        if name != "grad":
+            load.start()
     kc = nrhs // ncol
     front = minv.shape[1]
     width = minv.shape[0]
     ccols = cpl.shape[2]
     halves = width // LANES
 
-    loads = [
-        pltpu.make_async_copy(src, dst, load_sem.at[i])
-        for i, (src, dst) in enumerate(
-            [(inv_hbm, inv), (cpl_hbm, cpl), (minv_hbm, minv), (mcpl_hbm, mcpl), (rinv_hbm, rinv)]
+    barrier = pltpu.get_barrier_semaphore()
+
+    def wrap(i, n):
+        return jnp.where(i >= n, i - n, i)
+
+    near = [col] + [wrap(col + d, ncol) for d in range(1, ncol)]
+
+    def each(fn):
+        def step(t, _):
+            orow = wrap(row + t, nrow)
+            for d in range(ncol):
+                fn(orow, near[d])
+            return 0
+
+        lax.fori_loop(1, nrow, step, 0)
+        for d in range(1, ncol):
+            fn(row, near[d])
+
+    each(
+        lambda r, c: pl.semaphore_signal(
+            barrier, inc=1, device_id=(r, c), device_id_type=MESH
         )
-    ]
-    for load in loads:
-        load.start()
-
-    barrier = pltpu.get_barrier_semaphore()
-
-    def greet(t, _):
-        other = lax.rem(me + t, ndev)
-        pl.semaphore_signal(
-            barrier,
-            inc=1,
-            device_id=(lax.div(other, ncol), lax.rem(other, ncol)),
+    )
+
+    def send(phase, src, dst, r, c):
+        pltpu.make_async_remote_copy(
+            src_ref=src,
+            dst_ref=dst,
+            send_sem=send_sem.at[phase],
+            recv_sem=recv_sem.at[phase],
+            device_id=(r, c),
+            device_id_type=MESH,
+        ).start()
+
+    def to_all(phase, src_of, dst):
+        each(lambda r, c: send(phase, src_of(r * ncol + c, c), dst.at[me], r, c))
+
+    def to_rows(phase, src_of, dst):
+        def step(t, _):
+            orow = wrap(row + t, nrow)
+            send(phase, src_of(orow), dst.at[row], orow, col)
+            return 0
+
+        lax.fori_loop(1, nrow, step, 0, unroll=True)
+
+    def to_cols(phase, src_of, dst):
+        for d in range(1, ncol):
+            send(phase, src_of(near[d]), dst.at[col], row, near[d])
+
+    def leaf_copy(turn, f, src, dst, c, slot):
+        i = (turn * nleaf + f) * ncol
+        return pltpu.make_async_remote_copy(
+            src_ref=src,
+            dst_ref=dst.at[slot, f],
+            send_sem=send_leaf.at[i + c],
+            recv_sem=recv_leaf.at[i + slot],
+            device_id=(row, c),
             device_id_type=MESH,
         )
-        return 0
-
-    lax.fori_loop(1, ndev, greet, 0)
-
-    def to_all(phase, src_of, dst):
-        def step(t, _):
-            other = lax.rem(me + t, ndev)
-            orow, ocol = lax.div(other, ncol), lax.rem(other, ncol)
-            pltpu.make_async_remote_copy(
-                src_ref=src_of(other, ocol),
-                dst_ref=dst.at[me],
-                send_sem=send_sem.at[phase],
-                recv_sem=recv_sem.at[phase],
-                device_id=(orow, ocol),
-                device_id_type=MESH,
-            ).start()
-            return 0
-
-        lax.fori_loop(1, ndev, step, 0)
-
-    def to_rows(phase, src_of, dst):
-        def step(t, _):
-            orow = lax.rem(row + t, nrow)
-            pltpu.make_async_remote_copy(
-                src_ref=src_of(orow),
-                dst_ref=dst.at[row],
-                send_sem=send_sem.at[phase],
-                recv_sem=recv_sem.at[phase],
-                device_id=(orow, col),
-                device_id_type=MESH,
-            ).start()
-            return 0
-
-        lax.fori_loop(1, nrow, step, 0)
-
-    def to_cols(phase, src_of, dst):
-        def step(t, _):
-            ocol = lax.rem(col + t, ncol)
-            pltpu.make_async_remote_copy(
-                src_ref=src_of(ocol),
-                dst_ref=dst.at[col],
-                send_sem=send_sem.at[phase],
-                recv_sem=recv_sem.at[phase],
-                device_id=(row, ocol),
-                device_id_type=MESH,
-            ).start()
-            return 0
-
-        lax.fori_loop(1, ncol, step, 0)
 
     def arrive(phase, dst):
         part = dst.at[pl.ds(0, dst.shape[0] - 1)]
@@ -188,14 +216,21 @@
             axis=1,
         ).astype(BF16)
 
-    loads[0].wait()
+    loads["grad"].wait()
     for f in range(nleaf):
+        inv_loads[f].wait()
         part = dot(grad_ref[f], inv[f])
         for c in range(ncol):
             s_fwd[c, f] = part[:, c * share : (c + 1) * share].astype(BF16)
-    pl.semaphore_wait(barrier, ndev - 1)
-    to_cols(0, lambda c: s_fwd.at[c], r_fwd)
-    r_fwd[col] = s_fwd[col]
+        if f == 0:
+            pl.semaphore_wait(barrier, ndev - 1)
+        for c in range(1, ncol):
+
+            @pl.when(col < c)
+            def _():
+                leaf_copy(0, f, s_fwd.at[c, f], r_fwd, c, col).start()
+
+    loads["map"].wait()
 
     step_rows = 256
 
@@ -209,15 +244,26 @@
         return 0
 
     lax.fori_loop(0, front // step_rows, fill, 0)
+    loads["rgrad"].wait()
     rgrad[...] = rgrad_ref[...].astype(F32)
-    loads[1].wait()
-
-    arrive(0, r_fwd)
+    loads["cpl"].wait()
+    loads["size"].wait()
+    loads["parent"].wait()
+
     firsts = col * share + lax.broadcasted_iota(jnp.int32, (nrhs, share), 1)
     shares = []
     for f in range(nleaf):
-        y = r_fwd[0, f].astype(F32)
-        for c in range(1, ncol):
+        y = s_fwd[col, f].astype(F32)
+        for c in range(ncol - 1):
+
+            @pl.when(col > c)
+            def _():
+                leaf_copy(0, f, s_fwd.at[c, f], r_fwd, c, c).wait_recv()
+
+            @pl.when(col <= c)
+            def _():
+                r_fwd[c, f] = jnp.zeros((nrhs, share), BF16)
+
             y = y + r_fwd[c, f].astype(F32)
         y = jnp.where(firsts < size_ref[f], y, 0.0)
         leaf_y[f] = y
@@ -226,7 +272,7 @@
         s_cpl[c] = jnp.concatenate(
             [u[c * kc : (c + 1) * kc] for u in shares], axis=0
         ).astype(BF16)
-    to_cols(1, lambda c: s_cpl.at[c], r_cpl)
+    to_cols(0, lambda c: s_cpl.at[c], r_cpl)
     r_cpl[col] = s_cpl[col]
 
     def fill_mid(i, _):
@@ -235,12 +281,12 @@
         mpick[rows, :] = jnp.where(ids == mmap_ref[pl.ds(col, 1), :], 1.0, 0.0).astype(BF16)
         return 0
 
+    loads["mmap"].wait()
     lax.fori_loop(0, front // step_rows, fill_mid, 0)
-    loads[2].wait()
-    loads[3].wait()
-    loads[4].wait()
-
-    arrive(1, r_cpl)
+    for name in ("mgrad", "minv", "mcpl", "rinv"):
+        loads[name].wait()
+
+    arrive(0, r_cpl)
     u = r_cpl[0].astype(F32)
     for c in range(1, ncol):
         u = u + r_cpl[c].astype(F32)
@@ -258,10 +304,10 @@
         axis=1,
     ).astype(BF16)
     stage_blocks(s_con, dot_t(spread, pick[...]))
-    to_all(2, lambda d, c: s_con.at[d], r_con)
+    to_all(1, lambda d, c: s_con.at[d], r_con)
     r_con[me] = s_con[me]
 
-    arrive(2, r_con)
+    arrive(1, r_con)
     got = r_con[...].astype(F32).reshape(nrow, ncol, halves, kc, LANES)
     total = got[0]
     for r in range(1, nrow):
@@ -273,18 +319,18 @@
     part = dot(mid_hb, minv[...])
     for r in range(nrow):
         s_mid[r] = part[:, r * width : (r + 1) * width].astype(BF16)
-    to_rows(3, lambda r: s_mid.at[r], r_mid)
+    to_rows(2, lambda r: s_mid.at[r], r_mid)
     r_mid[row] = s_mid[row]
-    arrive(3, r_mid)
+    arrive(2, r_mid)
     mid_y = r_mid[0].astype(F32)
     for r in range(1, nrow):
         mid_y = mid_y + r_mid[r].astype(F32)
 
     mid_u = dot(mid_y.astype(BF16), mcpl[...])
     stage_blocks(s_root, dot_t(mid_u.astype(BF16), mpick[...]))
-    to_all(4, lambda d, c: s_root.at[d], r_root)
+    to_all(3, lambda d, c: s_root.at[d], r_root)
     r_root[me] = s_root[me]
-    arrive(4, r_root)
+    arrive(3, r_root)
     total = jnp.sum(r_root[...].astype(F32), axis=0)
     root_total = jnp.concatenate(
         [total[h * kc : (h + 1) * kc] for h in range(halves)], axis=1
@@ -294,21 +340,21 @@
     part = dot(root_hb, rinv[...])
     for r in range(nrow):
         s_ry[r] = pack(part[:, r * width : (r + 1) * width]).astype(BF16)
-    to_rows(5, lambda r: s_ry.at[r], r_ry)
+    to_rows(4, lambda r: s_ry.at[r], r_ry)
     r_ry[row] = s_ry[row]
-    arrive(5, r_ry)
+    arrive(4, r_ry)
     s_rg[...] = jnp.sum(r_ry[...].astype(F32), axis=0).astype(BF16)
-    to_rows(6, lambda r: s_rg, r_rg)
+    to_rows(5, lambda r: s_rg, r_rg)
     r_rg[row] = s_rg[...]
-    arrive(6, r_rg)
+    arrive(5, r_rg)
     ry = r_rg[...].astype(F32)
     root_yb = jnp.concatenate(
         [ry[r, h * kc : (h + 1) * kc] for r in range(nrow) for h in range(halves)], axis=1
     ).astype(BF16)
     s_rx[...] = pack(dot_t(root_yb, rinv[...])).astype(BF16)
-    to_all(7, lambda d, c: s_rx, r_rx)
+    to_all(6, lambda d, c: s_rx, r_rx)
     r_rx[me] = s_rx[...]
-    arrive(7, r_rx)
+    arrive(6, r_rx)
     root_xb = unpack_all(r_rx)
     own = r_rx[pl.ds(row * ncol, ncol)].astype(F32).reshape(ncol, halves, kc, LANES)
     for h in range(halves):
@@ -316,17 +362,17 @@
 
     coupled = dot(root_xb, mpick[...]).astype(BF16)
     s_mw[...] = (mid_y - dot_t(coupled, mcpl[...])).astype(BF16)
-    to_rows(8, lambda r: s_mw, r_mw)
+    to_rows(7, lambda r: s_mw, r_mw)
     r_mw[row] = s_mw[...]
-    arrive(8, r_mw)
+    arrive(7, r_mw)
     full_w = jnp.concatenate([r_mw[r] for r in range(nrow)], axis=1)
     mid_x = dot_t(full_w, minv[...])
     mid_out[...] = mid_x
     for c in range(ncol):
         s_mx[c] = pack(mid_x[c * kc : (c + 1) * kc]).astype(BF16)
-    to_all(9, lambda d, c: s_mx.at[c], r_mx)
+    to_all(8, lambda d, c: s_mx.at[c], r_mx)
     r_mx[me] = s_mx[col]
-    arrive(9, r_mx)
+    arrive(8, r_mx)
 
     every = dot(unpack_all(r_mx), pick[...])
     picked = []
@@ -337,9 +383,9 @@
             x = jnp.where(parent_ref[f] == p, every[p * kc : (p + 1) * kc, cols], x)
         picked.append(x)
     s_pk[...] = jnp.concatenate(picked, axis=0).astype(BF16)
-    to_cols(10, lambda c: s_pk, r_pk)
+    to_cols(9, lambda c: s_pk, r_pk)
     r_pk[col] = s_pk[...]
-    arrive(10, r_pk)
+    arrive(9, r_pk)
 
     got = r_pk[...].astype(F32)
     for f in range(nleaf):
@@ -348,17 +394,54 @@
         ).astype(BF16)
         w = leaf_y[f] - dot_t(xb, cpl[f])
         s_lw[f] = jnp.where(firsts < size_ref[f], w, 0.0).astype(BF16)
-    to_cols(11, lambda c: s_lw, r_lw)
-    r_lw[col] = s_lw[...]
-    arrive(11, r_lw)
+        for c in range(ncol - 1):
+
+            @pl.when(col > c)
+            def _():
+                leaf_copy(1, f, s_lw.at[f], r_lw, c, col).start()
+
     for f in range(nleaf):
+        r_lw[col, f] = s_lw[f]
+        for c in range(ncol):
+
+            @pl.when(col < c)
+            def _():
+                leaf_copy(1, f, s_lw.at[f], r_lw, c, c).wait_recv()
+
+            @pl.when(col > c)
+            def _():
+                r_lw[c, f] = jnp.zeros((nrhs, share), BF16)
+
         w = jnp.concatenate([r_lw[c, f] for c in range(ncol)], axis=1)
         leaf_out[f] = dot_t(w, inv[f])
 
+    for f in range(nleaf):
+        for c in range(ncol):
+
+            @pl.when(col < c)
+            def _():
+                leaf_copy(0, f, s_fwd.at[c, f], r_fwd, c, col).wait_send()
+
+            @pl.when(col > c)
+            def _():
+                leaf_copy(1, f, s_lw.at[f], r_lw, c, col).wait_send()
+
     for phase, buf in enumerate(
-        [r_fwd, r_cpl, r_con, r_mid, r_root, r_ry, r_rg, r_rx, r_mw, r_mx, r_pk, r_lw]
+        [r_cpl, r_con, r_mid, r_root, r_ry, r_rg, r_rx, r_mw, r_mx, r_pk]
     ):
         sent(phase, buf)
+
+
+def deliver(leaf, mid, root, leaf_out, mid_out, root_out, sem):
+    copies = [
+        pltpu.make_async_copy(leaf, leaf_out, sem.at[0]),
+        pltpu.make_async_copy(root, root_out, sem.at[1]),
+    ]
+    for copy in copies:
+        copy.start()
+    mid_out[...] = mid[...][:, None, :]
+    for copy in copies:
+        copy.wait()
 
 
 def fused(nrow, ncol, *args):
@@ -370,10 +453,14 @@
     width, front = mid_inv.shape[1:]
     ndev, kc, halves = nrow * ncol, nrhs // ncol, width // LANES
     vmem = pl.BlockSpec(memory_space=pltpu.VMEM)
-    smem = pl.BlockSpec(memory_space=pltpu.SMEM)
-    anyw = pl.BlockSpec(memory_space=pl.ANY)
+    hbm = pl.BlockSpec(memory_space=pltpu.HBM)
     block = (halves * kc, LANES)
     scratch = [
+        (leaf_grad.shape, BF16),
+        (leaf_map.shape, jnp.int32),
+        ((nrhs, width), BF16),
+        (mid_map.shape, jnp.int32),
+        (root_grad.shape, BF16),
         ((nleaf, share, order), BF16),
         ((nleaf, share, ccols), BF16),
         ((width, front), BF16),
@@ -408,7 +495,7 @@
         ((nleaf, nrhs, share), BF16),
         ((ncol, nleaf, nrhs, share), BF16),
     ]
-    phases = 12
+    phases = 10
     leaf_x, mid_x, root_x = pl.pallas_call(
         functools.partial(kernel, nrow, ncol),
         out_shape=(
@@ -416,22 +503,39 @@
             jax.ShapeDtypeStruct((nrhs, width), F32),
             jax.ShapeDtypeStruct((nrhs, width), F32),
         ),
-        in_specs=[vmem, anyw, anyw, smem, smem, vmem, vmem, anyw, anyw, vmem, vmem, anyw],
+        in_specs=[hbm] * 12,
         out_specs=(vmem, vmem, vmem),
         scratch_shapes=[pltpu.VMEM(shape, dtype) for shape, dtype in scratch]
         + [
-            pltpu.SemaphoreType.DMA((5,)),
+            pltpu.SMEM(leaf_size.shape, jnp.int32),
+            pltpu.SMEM(leaf_parent.shape, jnp.int32),
+            pltpu.SemaphoreType.DMA((11,)),
+            pltpu.SemaphoreType.DMA((nleaf,)),
             pltpu.SemaphoreType.DMA((phases,)),
             pltpu.SemaphoreType.DMA((phases,)),
+            pltpu.SemaphoreType.DMA((2 * nleaf * ncol,)),
+            pltpu.SemaphoreType.DMA((2 * nleaf * ncol,)),
         ],
         compiler_params=pltpu.CompilerParams(
-            collective_id=0, has_side_effects=True, vmem_limit_bytes=48 * 2**20
+            collective_id=0, has_side_effects=True, vmem_limit_bytes=63 * 2**20
         ),
     )(
         leaf_grad, leaf_inv, leaf_cpl, leaf_size, leaf_parent, leaf_map, mid_grad[:, 0, :],
         mid_inv[0], mid_cpl[0], mid_map, root_grad, root_inv,
     )
-    return leaf_x, mid_x[:, None, :], root_x
+    leaf_x, mid_x, root_x = pl.pallas_call(
+        deliver,
+        out_shape=(
+            jax.ShapeDtypeStruct(leaf_x.shape, F32),
+            jax.ShapeDtypeStruct((nrhs, 1, width), F32),
+            jax.ShapeDtypeStruct(root_x.shape, F32),
+        ),
+        in_specs=[pl.BlockSpec(memory_space=pl.ANY), vmem, pl.BlockSpec(memory_space=pl.ANY)],
+        out_specs=(hbm, vmem, hbm),
+        scratch_shapes=[pltpu.SemaphoreType.DMA((2,))],
+        compiler_params=pltpu.CompilerParams(vmem_limit_bytes=63 * 2**20),
+    )(leaf_x, mid_x, root_x)
+    return leaf_x, mid_x, root_x
 
 
 def body(

time: 84.3 us -> 78.9 us (0.936)
  local copies, waits for them, and re-layouts: 13.1 us -> 0 us
  Pallas kernels: 69.7 us -> 78.1 us
    unnamed x27 -> x0, local copies, waits for them, and re-layouts: 13.1 us -> none
    pallas_call x0 -> x1, Pallas kernels: none -> 7.45 us  [fused(): pl.pallas_call(deliver, out_shape=(jax.ShapeDtypeStruct(leaf_x.shape, F32...]
    pallas_call x1, Pallas kernels: 69.7 us -> 70.6 us  [fused(): pl.pallas_call(functools.partial(kernel, nrow, ncol), out_shape=(jax.Shap...]
where the time goes in v2:
time: 78.9 us; the launch traced here: 78.7 us
  Pallas kernels  78.1 us (99%)
    pallas_call x1, Pallas kernels, fused(): pl.pallas_call(functools.partial(kernel, nrow, ncol), out_shape=(jax.Shap...  70.6 us
    pallas_call x1, Pallas kernels, fused(): pl.pallas_call(deliver, out_shape=(jax.ShapeDtypeStruct(leaf_x.shape, F32...  7.45 us

profile of v2, /device:TPU:0, one launch (start us, length us, event | category | flops | bytes accessed | tf_op | source)
XLA Modules:
  0.0 78.7 jit_solution(4966943645522857955)
XLA Ops:
  0.6 70.6 %shard_map.139 = (f32[4,32,256]{2,1,0:T(8,128)}, f32[32,256]{1,0:T(8,128)}, f32[32,256]{1,0:T(8,128)}) custom-call(bf16[4,32,256]{2,1,0:T(8,128)(2,1)} %grad_hbm.1, bf16[4,256,1024]{2,1,0:T(8,128)(2,1)} %inv_hbm.1, bf16[4,256,512]{2,1,0:T(8,128)(2,1)} %cpl_hbm.1, s32[4]{0:T(128)} %size_hbm.1, s32[4]{0:T(128)} %parent_hbm.1, s32[4,512]{1,0:T(4,128)} %map_hbm.1, ...), custom_call_target="tpu_custom_call" | custom-call | tf_op jit(solution)/shard_map/pallas_call | solution.py:499
  71.3 7.5 %shard_map.140 = (f32[4,32,256]{2,1,0:T(8,128)}, f32[32,1,256]{2,1,0:T(1,128)}, f32[32,256]{1,0:T(8,128)}) custom-call(f32[4,32,256]{2,1,0:T(8,128)} %get-tuple-element.6.leaf, f32[32,256]{1,0:T(8,128)} %get-tuple-element.7.mid, f32[32,256]{1,0:T(8,128)} %get-tuple-element.8.root), custom_call_target="tpu_custom_call" | custom-call | tf_op jit(solution)/shard_map/pallas_call | solution.py:526
